TPU v7x, 128 devices: a whole 4x4x4 slice. The times are simulated.
128 devices in a mesh: gx: 32 (over y, x_lo, z), gy: 4 (over x_hi, core).
Axes of the slice: x: 4 (x_hi: 2, x_lo: 2; x = x_hi * 2 + x_lo), y: 4, z: 4, core: 2. Of those that a mesh axis runs over, the one named last changes fastest.
Arguments:
- embeddings: bfloat16 [32, 512, 768], P('gy', 'gx'), may hold values from -6 to 6
- tile_valid: int32 [32, 512], P('gy', 'gx'), may hold values 0 or 1
- w_query: bfloat16 [768, 768], replicated, may hold values from -0.4375 to 0.4375
- w_key: bfloat16 [768, 768], replicated, may hold values from -0.21875 to 0.21875
- w_value: bfloat16 [768, 768], replicated, may hold values from -0.21875 to 0.21875
- w_out: bfloat16 [768, 768], replicated, may hold values from -1.25 to 1.25
- w_up: bfloat16 [768, 3072], replicated, may hold values from -0.21875 to 0.21875
- w_down: bfloat16 [3072, 768], replicated, may hold values from -0.109375 to 0.109375
- gain_attn: float32 [768], replicated, may hold values from 0.25 to 1.75
- shift_attn: float32 [768], replicated, may hold values from -4 to 4
- gain_mlp: float32 [768], replicated, may hold values from 0.25 to 1.75
- shift_mlp: float32 [768], replicated, may hold values from -4 to 4
- cotangent: bfloat16 [32, 512, 768], P('gy', 'gx'), may hold values from -6 to 6
Outputs:
- mixed: bfloat16 [32, 512, 768], P('gy', 'gx')
- grad_embeddings: float32 [32, 512, 768], P('gy', 'gx')
- grad_w_query: float32 [768, 768], replicated
- grad_w_key: float32 [768, 768], replicated
- grad_w_value: float32 [768, 768], replicated
- grad_w_out: float32 [768, 768], replicated
- grad_w_up: float32 [768, 3072], replicated
- grad_w_down: float32 [3072, 768], replicated
- grad_gain_attn: float32 [768], replicated
- grad_shift_attn: float32 [768], replicated
- grad_gain_mlp: float32 [768], replicated
- grad_shift_mlp: float32 [768], replicated
All inputs are finite; a program needn't handle non-finite values. No bound on the sum of `tile_valid` on one device may be relied on, other than what follows from the above.
Results may differ from a plain program's by a relative error of at most 0.014.
The roundings to bfloat16 on the way count: a program that leaves them out, or rounds other values in their place, can miss the bound.
Values may be sent and summed in bfloat16 or wider, within the bound.
No kernel may reach another device: no remote copies, remote signals or barrier semaphores. Data moves between devices by JAX's collectives and lax.ppermute only.
A program may use at most 192 MiB of HBM per device.

v0:
```python
import math

import jax
import jax.numpy as jnp
from jax import lax
from jax.sharding import PartitionSpec as P

HEADS = 16
STRIDE = 4


epsilon = 1e-05
group_width = 2


def passed_along(value, axis, steps):
    count = lax.axis_size(axis)
    first, last = (max(0, -steps), min(count, count - steps))
    return lax.ppermute(value, axis, [(source, source + steps) for source in range(first, last)])


def padded(cells, sides, width):
    for axis, dim in sides:
        count = lax.axis_size(axis)
        ends = count - 1
        head = lax.slice_in_dim(cells, 0, width, axis=dim)
        tail = lax.slice_in_dim(cells, cells.shape[dim] - width, cells.shape[dim], axis=dim)
        cells = jnp.concatenate(
            [
                lax.ppermute(tail, axis, [(i, (i + 1) % count) for i in range(ends)]),
                cells,
                lax.ppermute(head, axis, [((i + 1) % count, i) for i in range(ends)]),
            ],
            axis=dim,
        )
    return cells


def layer_norm(inputs, gain_vec, shift_vec):
    row_mean = jnp.mean(inputs, axis=-1, keepdims=True)
    centered = inputs - row_mean
    row_var = jnp.mean(centered * centered, axis=-1, keepdims=True)
    return centered * lax.rsqrt(row_var + epsilon) * gain_vec + shift_vec


def exact_gelu(inputs):
    return jax.nn.gelu(inputs, approximate=False)


def product(left_op, right_op):
    return jnp.dot(left_op, right_op, preferred_element_type=jnp.float32)


def window_weights(key_flags, block_rows, block_cols, margin):
    reg_cols = block_cols + 2 * margin
    query_pos = jnp.arange(block_rows * block_cols)
    key_pos = jnp.arange(key_flags.shape[0])
    row_gap = (key_pos // reg_cols - margin)[None, :] - (query_pos // block_cols)[:, None]
    col_gap = (key_pos % reg_cols - margin)[None, :] - (query_pos % block_cols)[:, None]
    dense = (jnp.abs(row_gap) <= margin) & (jnp.abs(col_gap) <= margin)
    dilated = dense & (row_gap % 2 == 0) & (col_gap % 2 == 0)
    itself = (row_gap == 0) & (col_gap == 0)
    counted = jnp.where(itself, 1.0, key_flags[None, :])
    return (dense.astype(key_flags.dtype) + dilated.astype(key_flags.dtype)) * counted


def masked_scores(queries, key_rows, pair_weights, score_scale):
    raw_scores = (
        jnp.einsum("qhd,khd->hqk", queries, key_rows, preferred_element_type=jnp.float32)
        * score_scale
    )
    return jnp.where(pair_weights[None] > 0, raw_scores, -1e30)


def heads_of(array, group_index):
    return lax.dynamic_slice_in_dim(array, group_index * group_width, group_width, 1)


def return_columns(strip, offset):
    return passed_along(strip.astype(jnp.bfloat16), "gx", offset).astype(strip.dtype)


def return_rows(strip, offset):
    return passed_along(strip.astype(jnp.bfloat16), "gy", offset).astype(strip.dtype)


def fold_margins(grad_pair, block_rows, block_cols, margin):
    left_strip = grad_pair[:, :margin]
    right_strip = grad_pair[:, margin + block_cols :]
    centre = grad_pair[:, margin : margin + block_cols]
    centre = centre.at[:, block_cols - margin :].add(return_columns(left_strip, -1))
    centre = centre.at[:, :margin].add(return_columns(right_strip, 1))
    top_strip = centre[:margin]
    bottom_strip = centre[margin + block_rows :]
    middle = centre[margin : margin + block_rows]
    middle = middle.at[block_rows - margin :].add(return_rows(top_strip, -1))
    middle = middle.at[:margin].add(return_rows(bottom_strip, 1))
    return middle


def local(
    embeddings,
    tile_valid,
    w_query,
    w_key,
    w_value,
    w_out,
    w_up,
    w_down,
    gain_attn,
    shift_attn,
    gain_mlp,
    shift_mlp,
    cotangent,
):
    block_rows, block_cols, model_width = embeddings.shape
    tokens = block_rows * block_cols
    head_count = HEADS
    head_dim = model_width // head_count
    margin = min(16, min(block_rows, block_cols))
    stride = STRIDE
    score_scale = 1.0 / math.sqrt(head_dim)
    reg_rows = block_rows + 2 * margin
    reg_cols = block_cols + 2 * margin
    residual = embeddings.astype(jnp.float32).reshape(tokens, model_width)
    normed_attn, attn_norm_back = jax.vjp(layer_norm, residual, gain_attn, shift_attn)
    act_attn = normed_attn.astype(jnp.bfloat16)
    queries = product(act_attn, w_query).astype(jnp.bfloat16)
    key_rows = product(act_attn, w_key).astype(jnp.bfloat16)
    value_rows = product(act_attn, w_value).astype(jnp.bfloat16)
    key_flags = tile_valid.astype(jnp.bfloat16)
    key_block = key_rows.reshape(block_rows, block_cols, model_width)
    value_block = value_rows.reshape(block_rows, block_cols, model_width)
    key_region, value_region, flag_region = (
        padded(key_block, (("gx", 1), ("gy", 0)), margin),
        padded(value_block, (("gx", 1), ("gy", 0)), margin),
        padded(key_flags, (("gx", 1), ("gy", 0)), margin),
    )
    near_keys = key_region.reshape(reg_rows * reg_cols, model_width)
    near_values = value_region.reshape(reg_rows * reg_cols, model_width)
    spaced_rows = block_rows // stride
    spaced_cols = block_cols // stride
    spaced_keys = key_block[::stride, ::stride].reshape(spaced_rows * spaced_cols, model_width)
    spaced_values = value_block[::stride, ::stride].reshape(spaced_rows * spaced_cols, model_width)
    spaced_flags = key_flags[::stride, ::stride].reshape(spaced_rows * spaced_cols)
    far_keys, far_values, far_flags = (
        lax.all_gather(spaced_keys, ("gx", "gy"), axis=0, tiled=True),
        lax.all_gather(spaced_values, ("gx", "gy"), axis=0, tiled=True),
        lax.all_gather(spaced_flags, ("gx", "gy"), axis=0, tiled=True),
    )
    local_count = reg_rows * reg_cols
    far_count = far_keys.shape[0]
    all_keys = jnp.concatenate([near_keys, far_keys], axis=0).reshape(
        local_count + far_count, head_count, head_dim
    )
    all_values = jnp.concatenate([near_values, far_values], axis=0).reshape(
        local_count + far_count, head_count, head_dim
    )
    pair_weights = jnp.concatenate(
        [
            window_weights(
                flag_region.reshape(local_count).astype(jnp.float32), block_rows, block_cols, margin
            ),
            jnp.broadcast_to(far_flags.astype(jnp.float32)[None, :], (tokens, far_count)),
        ],
        axis=1,
    )
    query_heads = queries.reshape(tokens, head_count, head_dim)
    groups = jnp.arange(head_count // group_width, dtype=jnp.int32)

    def forward_group(group_index):
        query_part = heads_of(query_heads, group_index)
        key_part = heads_of(all_keys, group_index)
        value_part = heads_of(all_values, group_index)
        masked = masked_scores(query_part, key_part, pair_weights, score_scale)
        row_top = jnp.max(masked, axis=2, keepdims=True)
        weighted = pair_weights[None] * jnp.exp(masked - row_top)
        row_total = jnp.sum(weighted, axis=2, keepdims=True)
        attn_probs = (weighted / row_total).astype(jnp.bfloat16)
        attn_out = jnp.einsum(
            "hqk,khd->qhd", attn_probs, value_part, preferred_element_type=jnp.float32
        )
        return (attn_out.astype(jnp.bfloat16), row_top + jnp.log(row_total))

    group_outs, log_totals = lax.map(forward_group, groups)
    attended = group_outs.transpose(1, 0, 2, 3).reshape(tokens, model_width)
    middle = residual + product(attended, w_out)
    normed_mlp, mlp_norm_back = jax.vjp(layer_norm, middle, gain_mlp, shift_mlp)
    act_mlp = normed_mlp.astype(jnp.bfloat16)
    pre_act = product(act_mlp, w_up)
    gelu_out, gelu_back = jax.vjp(exact_gelu, pre_act)
    hidden = gelu_out.astype(jnp.bfloat16)
    output = middle + product(hidden, w_down)
    grad_out = cotangent.reshape(tokens, model_width)
    grad_down = product(hidden.T, grad_out)
    grad_hidden = product(grad_out, w_down.T)
    grad_pre = gelu_back(grad_hidden)[0].astype(jnp.bfloat16)
    grad_up = product(act_mlp.T, grad_pre)
    grad_act_mlp = product(grad_pre, w_up.T)
    grad_mid_norm, grad_gain_mlp, grad_shift_mlp = mlp_norm_back(grad_act_mlp)
    grad_mid = grad_out.astype(jnp.float32) + grad_mid_norm
    grad_branch = grad_mid.astype(jnp.bfloat16)
    grad_wout = product(attended.T, grad_branch)
    grad_att = (
        product(grad_branch, w_out.T).astype(jnp.bfloat16).reshape(tokens, head_count, head_dim)
    )

    def backward_group(group_pair):
        group_index, log_total = group_pair
        query_part = heads_of(query_heads, group_index)
        key_part = heads_of(all_keys, group_index)
        value_part = heads_of(all_values, group_index)
        grad_part = heads_of(grad_att, group_index)
        masked = masked_scores(query_part, key_part, pair_weights, score_scale)
        attn_probs = pair_weights[None] * jnp.exp(masked - log_total)
        grad_prob = jnp.einsum(
            "qhd,khd->hqk", grad_part, value_part, preferred_element_type=jnp.float32
        )
        row_inner = jnp.sum(attn_probs * grad_prob, axis=2, keepdims=True)
        grad_score = (attn_probs * (grad_prob - row_inner)).astype(jnp.bfloat16)
        grad_q = (
            jnp.einsum("hqk,khd->qhd", grad_score, key_part, preferred_element_type=jnp.float32)
            * score_scale
        )
        grad_k = (
            jnp.einsum("hqk,qhd->khd", grad_score, query_part, preferred_element_type=jnp.float32)
            * score_scale
        )
        grad_v = jnp.einsum(
            "hqk,qhd->khd",
            attn_probs.astype(jnp.bfloat16),
            grad_part,
            preferred_element_type=jnp.float32,
        )
        return (grad_q, grad_k, grad_v)

    grad_q_groups, grad_k_groups, grad_v_groups = lax.map(backward_group, (groups, log_totals))
    grad_query = (
        grad_q_groups.transpose(1, 0, 2, 3).reshape(tokens, model_width).astype(jnp.bfloat16)
    )
    grad_keys_all = grad_k_groups.transpose(1, 0, 2, 3).reshape(
        local_count + far_count, model_width
    )
    grad_values_all = grad_v_groups.transpose(1, 0, 2, 3).reshape(
        local_count + far_count, model_width
    )
    far_key_grad, far_value_grad = (
        lax.psum_scatter(
            grad_keys_all[local_count:], ("gx", "gy"), scatter_dimension=0, tiled=True
        ),
        lax.psum_scatter(
            grad_values_all[local_count:], ("gx", "gy"), scatter_dimension=0, tiled=True
        ),
    )
    grad_pair = jnp.stack(
        [
            grad_keys_all[:local_count].reshape(reg_rows, reg_cols, model_width),
            grad_values_all[:local_count].reshape(reg_rows, reg_cols, model_width),
        ],
        axis=2,
    )
    near_grads = fold_margins(grad_pair, block_rows, block_cols, margin)

    def add_spaced(block_grad, addition):
        shaped = block_grad.reshape(spaced_rows, stride, spaced_cols, stride, model_width)
        shaped = shaped.at[:, 0, :, 0].add(addition.reshape(spaced_rows, spaced_cols, model_width))
        return shaped.reshape(tokens, model_width)

    grad_key = add_spaced(near_grads[:, :, 0], far_key_grad).astype(jnp.bfloat16)
    grad_value = add_spaced(near_grads[:, :, 1], far_value_grad).astype(jnp.bfloat16)
    grad_wq = product(act_attn.T, grad_query)
    grad_wk = product(act_attn.T, grad_key)
    grad_wv = product(act_attn.T, grad_value)
    grad_act_attn = (
        product(grad_query, w_query.T) + product(grad_key, w_key.T) + product(grad_value, w_value.T)
    )
    grad_in_norm, grad_gain_attn, grad_shift_attn = attn_norm_back(grad_act_attn)
    grad_inputs = grad_mid + grad_in_norm
    (
        grad_wq,
        grad_wk,
        grad_wv,
        grad_wout,
        grad_up,
        grad_down,
        grad_gain_attn,
        grad_shift_attn,
        grad_gain_mlp,
        grad_shift_mlp,
    ) = lax.psum(
        (
            grad_wq,
            grad_wk,
            grad_wv,
            grad_wout,
            grad_up,
            grad_down,
            grad_gain_attn,
            grad_shift_attn,
            grad_gain_mlp,
            grad_shift_mlp,
        ),
        ("gx", "gy"),
    )
    mixed = output.astype(jnp.bfloat16).reshape(block_rows, block_cols, model_width)
    grad_embeddings = grad_inputs.reshape(block_rows, block_cols, model_width)
    return (
        mixed,
        grad_embeddings,
        grad_wq,
        grad_wk,
        grad_wv,
        grad_wout,
        grad_up,
        grad_down,
        grad_gain_attn,
        grad_shift_attn,
        grad_gain_mlp,
        grad_shift_mlp,
    )


def solution(mesh):
    in_specs = (
        P("gy", "gx", None),
        P("gy", "gx"),
        P(),
        P(),
        P(),
        P(),
        P(),
        P(),
        P(),
        P(),
        P(),
        P(),
        P("gy", "gx", None),
    )
    out_specs = (
        P("gy", "gx", None),
        P("gy", "gx", None),
        P(),
        P(),
        P(),
        P(),
        P(),
        P(),
        P(),
        P(),
        P(),
        P(),
    )
    return jax.shard_map(local, mesh=mesh, in_specs=in_specs, out_specs=out_specs, check_vma=False)
```

profile of v0, /device:TPU:1, one launch (start us, length us, event | category | flops | bytes accessed | tf_op | source)
XLA Modules:
  0.0 2119.4 jit_solution(17384756546243700077)
XLA Ops:
  14.5 4.4 collective-permute-start.4
  20.8 4.2 collective-permute-start
  27.0 4.0 collective-permute-start.8
  31.3 71.6 %all-reduce = bf16[1024]{0:T(1024)(128)(2,1)S(1)} all-reduce(bf16[1024]{0:T(1024)(128)(2,1)S(1)} %dynamic-update-slice.16), channel_id=1, replica_groups=mesh['gx'=32,'gy'=4] {'gx','gy'}, use_global_device_ids=true, to_apply=%add | all-reduce | flops 1024 | bytes 4096
  103.3 2.6 collective-permute-start.7
  106.0 4.5 collective-permute-start.6
  115.4 5.1 collective-permute-start.2
  122.6 5.1 collective-permute-start.10
  127.8 3.6 collective-permute-done.11
  134.7 5.7 concatenate.59
  140.4 4.8 copy.63
  145.3 2.2 pad_maximum_fusion.2
  147.5 5.7 concatenate.51
  153.3 4.8 copy.60
  158.1 54.4 %all-gather.5.cloned.1.call-done = bf16[1024,768]{1,0:T(8,128)(2,1)} async-done(((bf16[8,768]{1,0:T(8,128)(2,1)}), bf16[1024,768]{1,0:T(8,128)(2,1)}) %all-gather.5.cloned.1.call-update) | async-done | bytes 1572880 | tf_op jit(solution)/shard_map/all_gather | solution.py:147
  212.6 2.6 copy.62
  215.1 191.4 %all-gather.3.cloned.1.call-done = bf16[1024,768]{1,0:T(8,128)(2,1)} async-done(((bf16[8,768]{1,0:T(8,128)(2,1)}), bf16[1024,768]{1,0:T(8,128)(2,1)}) %all-gather.3.cloned.1.call-update) | async-done | bytes 1572880 | tf_op jit(solution)/shard_map/all_gather | solution.py:148
  406.5 2.6 copy.59
  409.1 4.3 pad_maximum_fusion
  413.5 41.2 %while.34 = (s32[]{:T(128)}, bf16[8,128,2,48]{1,3,2,0:T(8,128)(2,1)S(1)}, f32[8,2,128,1]{2,1,3,0:T(2,128)S(1)}, s32[8]{0:T(128)S(1)}, bf16[1792,16,48]{0,2,1:T(8...) while((s32[]{:T(128)}, ...), condition=%wide.region_5.6_spmd, body=%wide.region_2.5_spmd.sunk | while | flops 92909312 | bytes 9462979 | solution.py:185
  457.3 3.3 fusion.67
  460.7 8.5 add_convert_fusion
  474.6 80.6 %while.35 = (s32[]{:T(128)}, bf16[8,128,2,48]{1,3,2,0:T(8,128)(2,1)}, f32[8,1792,2,48]{1,3,2,0:T(8,128)}, f32[8,1792,2,48]{1,3,2,0:T(8,128)}, s32[8]{0:T(128)S(1...) while((s32[]{:T(128)}, ...), condition=%wide.region_12.13_spmd, body=%wide.region_10.12_spmd.sunk | while | flops 225201920 | bytes 18619628 | solution.py:237
  477.5 2.0 multiply_reduce_fusion.8
  479.7 2.0 fusion.152
  487.5 2.0 multiply_reduce_fusion.8
  489.8 2.0 fusion.152
  497.6 2.0 multiply_reduce_fusion.8
  499.9 2.0 fusion.152
  507.7 2.0 multiply_reduce_fusion.8
  509.9 2.0 fusion.152
  517.7 2.0 multiply_reduce_fusion.8
  520.0 2.0 fusion.152
  527.8 2.0 multiply_reduce_fusion.8
  530.1 2.0 fusion.152
  537.9 2.0 multiply_reduce_fusion.8
  540.1 2.0 fusion.152
  548.0 2.0 multiply_reduce_fusion.8
  550.2 2.0 fusion.152
  555.2 4.0 slice.296
  559.2 3.5 copy.69
  562.8 4.0 slice.293
  566.8 3.6 copy.67
  571.3 3.3 slice.282
  574.5 3.3 slice.281
  577.8 9.5 copy.65
  587.3 11.7 stack_reshape.6
  599.0 9.3 copy.66
  608.3 11.7 stack_reshape.7
  620.1 2.0 constant_dynamic-update-slice_fusion.2
  625.7 5.3 fusion.66
  631.2 4.1 collective-permute-start.13
  639.3 7.5 collective-permute-done.13
  647.3 4.4 collective-permute-start.14
  651.7 3.4 collective-permute-start.15
  655.2 5.2 fusion.84
  665.1 532.9 %reduce-scatter.5.cloned.1.call-done = f32[8,768]{1,0:T(8,128)} async-done(((f32[1024,768]{1,0:T(8,128)}), f32[8,768]{1,0:T(8,128)}) %reduce-scatter.5.cloned.1.call-update) | async-done | bytes 24592 | tf_op jit(solution)/shard_map/reduce_scatter | solution.py:251
  1204.2 632.6 %reduce-scatter.3.cloned.1.call-done = f32[8,768]{1,0:T(8,128)} async-done(((f32[1024,768]{1,0:T(8,128)}), f32[8,768]{1,0:T(8,128)}) %reduce-scatter.3.cloned.1.call-update) | async-done | bytes 24592 | tf_op jit(solution)/shard_map/reduce_scatter | solution.py:248
  1850.0 3.9 fusion.41
  1855.5 71.1 %all-reduce.1 = (f32[768]{0:T(1024)}, f32[768]{0:T(1024)}, f32[768]{0:T(1024)}, f32[768]{0:T(1024)}) all-reduce(f32[768]{0:T(1024)S(1)} %get-tuple-element.228, f32[768]{0:T(1024)S(1)} %get-tuple-element.231, f32[768]{0:T(1024)S(1)} %get-tuple-element.226, f32[768]{0:T(1024)S(1)} %get-tuple-element.230), channel_id=1, replica_groups=mesh['gx'=32,'gy'=4] {'gx','gy'}, use_global_device_ids=true, to_apply=%region_24.25 | all-reduce | flops 3072 | bytes 24576 | tf_op jit(solution)/shard_map/psum | solution.py:290
  1927.5 162.0 %all-reduce.5.cloned.1.call-done = (f32[768,768]{1,0:T(8,128)}, f32[768,768]{1,0:T(8,128)}, f32[768,768]{1,0:T(8,128)}, f32[768,768]{1,0:T(8,128)}, f32[768,3072]{1,0:T(8,128)}, /*index=5*/f32[3072,768]{1,0:T(8,128)}) async-done(((f32[768,768]{1,0:T(8,128)}, f32[768,768]{1,0:T(8,128)}, f32[768,768]{1,0:T(8,128)}, f32[768,768]{1,0:T(8,128)}, f32[768,3072]{1,0:T(8,128)}, /*index=5*/f32[3072,768]{1,0:T(8,128)}), ...) | async-done | bytes 28311568 | tf_op jit(solution)/shard_map/psum | solution.py:290
  2089.5 3.4 copy.109
  2099.3 9.3 copy.113
  2108.6 3.7 copy.114
  (297 shorter events, 150.4 us)
Async XLA Ops:
  7.2 6.1 copy-start
  7.2 205.4 %all-gather.5.cloned.1.call-start = ((), (), s32[]{:S(2)}) async-start(), calls=%async_computation.3 | async-start | bytes 1585152 | tf_op jit(solution)/shard_map/all_gather | solution.py:147
  10.8 3.6 copy-start.29
  12.4 90.5 %copy-start.6 = (bf16[768,768]{1,0:T(8,128)(2,1)S(1)}, bf16[768,768]{1,0:T(8,128)(2,1)}, u32[]{:S(2)}) copy-start(bf16[768,768]{1,0:T(8,128)(2,1)} %param.35) | copy-start | bytes 3538948
  13.2 393.4 %all-gather.3.cloned.1.call-start = ((), (), s32[]{:S(2)}) async-start(), calls=%async_computation.2 | async-start | bytes 1585152 | tf_op jit(solution)/shard_map/all_gather | solution.py:148
  14.3 1183.8 %reduce-scatter.5.cloned.1.call-start = ((), (), s32[]{:S(2)}) async-start(), calls=%async_computation.5 | async-start | bytes 3170304 | tf_op jit(solution)/shard_map/reduce_scatter | solution.py:251
  14.5 88.8 %collective-permute-start.4 = (bf16[8,8]{1,0:T(8,128)(2,1)S(1)}, bf16[8,8]{1,0:T(8,128)(2,1)S(1)}, u32[]{:S(2)}, u32[]{:S(2)}) collective-permute-start(bf16[8,8]{1,0:T(8,128)(2,1)S(1)} %get-tuple-element.301), channel_id=1, source_target_pairs={{0,4},{4,8},{8,12},{12,16},{16,20},{20,24},{24,28},{28,32},{32,36}... | collective-permute-start | bytes 392 | tf_op jit(solution)/shard_map/ppermute | solution.py:30
  18.8 84.4 %collective-permute-start.5 = (bf16[8,8]{1,0:T(8,128)(2,1)S(1)}, bf16[8,8]{1,0:T(8,128)(2,1)S(1)}, u32[]{:S(2)}, u32[]{:S(2)}) collective-permute-start(bf16[8,8]{1,0:T(8,128)(2,1)S(1)} %get-tuple-element.302), channel_id=1, source_target_pairs={{4,0},{8,4},{12,8},{16,12},{20,16},{24,20},{28,24},{32,28},{36,32}... | collective-permute-start | bytes 392 | tf_op jit(solution)/shard_map/ppermute | solution.py:32
  20.8 91.9 %collective-permute-start = (bf16[8,8,768]{2,1,0:T(8,128)(2,1)}, bf16[8,8,768]{2,1,0:T(8,128)(2,1)S(1)}, u32[]{:S(2)}, u32[]{:S(2)}) collective-permute-start(bf16[8,8,768]{2,1,0:T(8,128)(2,1)} %get-tuple-element.297), channel_id=1, source_target_pairs={{0,4},{4,8},{8,12},{12,16},{16,20},{20,24},{24,28},{28,32},{32,36}... | collective-permute-start | bytes 294920 | tf_op jit(solution)/shard_map/ppermute | solution.py:30
  25.0 87.7 %collective-permute-start.1 = (bf16[8,8,768]{2,1,0:T(8,128)(2,1)}, bf16[8,8,768]{2,1,0:T(8,128)(2,1)S(1)}, u32[]{:S(2)}, u32[]{:S(2)}) collective-permute-start(bf16[8,8,768]{2,1,0:T(8,128)(2,1)} %get-tuple-element.298), channel_id=1, source_target_pairs={{4,0},{8,4},{12,8},{16,12},{20,16},{24,20},{28,24},{32,28},{36,32}... | collective-permute-start | bytes 294920 | tf_op jit(solution)/shard_map/ppermute | solution.py:32
  27.0 93.6 %collective-permute-start.8 = (bf16[8,8,768]{2,1,0:T(8,128)(2,1)}, bf16[8,8,768]{2,1,0:T(8,128)(2,1)S(1)}, u32[]{:S(2)}, u32[]{:S(2)}) collective-permute-start(bf16[8,8,768]{2,1,0:T(8,128)(2,1)} %get-tuple-element.295), channel_id=1, source_target_pairs={{0,4},{4,8},{8,12},{12,16},{16,20},{20,24},{24,28},{28,32},{32,36}... | collective-permute-start | bytes 294920 | tf_op jit(solution)/shard_map/ppermute | solution.py:30
  103.3 7.3 collective-permute-start.7
  106.0 6.0 collective-permute-start.6
  110.7 10.0 collective-permute-start.9
  113.5 31.8 %collective-permute-start.3 = (bf16[8,32,768]{2,1,0:T(8,128)(2,1)}, bf16[8,32,768]{2,1,0:T(8,128)(2,1)}, u32[]{:S(2)}, u32[]{:S(2)}) collective-permute-start(bf16[8,32,768]{2,1,0:T(8,128)(2,1)} %pad_maximum_fusion.5), channel_id=1, source_target_pairs={{1,0},{2,1},{3,2},{5,4},{6,5},{7,6},{9,8},{10,9},{11,10},{13,12},{... | collective-permute-start | bytes 1179656 | tf_op jit(solution)/shard_map/ppermute | solution.py:32
  115.4 29.8 %collective-permute-start.2 = (bf16[8,32,768]{2,1,0:T(8,128)(2,1)}, bf16[8,32,768]{2,1,0:T(8,128)(2,1)}, u32[]{:S(2)}, u32[]{:S(2)}) collective-permute-start(bf16[8,32,768]{2,1,0:T(8,128)(2,1)} %pad_maximum_fusion.5), channel_id=1, source_target_pairs={{0,1},{1,2},{2,3},{4,5},{5,6},{6,7},{8,9},{9,10},{10,11},{12,13},{... | collective-permute-start | bytes 1179656 | tf_op jit(solution)/shard_map/ppermute | solution.py:30
  120.6 2.0 copy-start.24
  120.7 10.8 collective-permute-start.11
  122.6 10.1 collective-permute-start.10
  413.5 41.9 %copy-start.1 = (bf16[8,16,768]{2,1,0:T(8,128)(2,1)S(1)}, bf16[8,16,768]{2,1,0:T(8,128)(2,1)}, u32[]{:S(2)}) copy-start(bf16[8,16,768]{2,1,0:T(8,128)(2,1)} %param.33) | copy-start | bytes 589828
  454.7 0.7 copy-start.18
  454.7 6.0 copy-start.22
  454.7 2.6 copy-start.25
  454.7 2.6 copy-start.27
  457.3 3.4 copy-start.15
  457.3 11.9 slice-start
  460.7 8.5 copy-start.3
  460.7 8.5 slice-start.1
  469.2 1.8 copy-start.8
  471.0 1.3 copy-start.5
  562.7 1274.0 %reduce-scatter.3.cloned.1.call-start = ((), (), s32[]{:S(2)}) async-start(), calls=%async_computation.4 | async-start | bytes 3170304 | tf_op jit(solution)/shard_map/reduce_scatter | solution.py:248
  570.4 0.7 copy-start.26
  570.4 0.7 copy-start.28
  570.4 1519.1 %all-reduce.5.cloned.1.call-start = ((), (), s32[]{:S(2)}) async-start(), calls=%async_computation.6 | async-start | bytes 56623104 | tf_op jit(solution)/shard_map/psum | solution.py:290
  620.1 2.4 copy-start.2
  622.6 1.9 copy-start.19
  623.0 1.6 copy-start.4
  623.1 16.0 collective-permute-start.12
  624.6 1.1 copy-start.9
  631.0 4.3 copy-start.23
  631.2 6.0 copy-start.20
  631.2 15.6 collective-permute-start.13
  647.3 7.9 copy-start.16
  647.3 13.0 collective-permute-start.14
  651.7 8.6 collective-permute-start.15
  1843.5 1.9 copy-start.13
  1847.3 0.9 copy-start.21
  1850.0 3.9 copy-start.7
  1850.0 3.9 copy-start.14
  1854.5 72.0 %copy-start.17 = (bf16[8,16,768]{2,1,0:T(8,128)(2,1)S(1)}, bf16[8,16,768]{2,1,0:T(8,128)(2,1)}, u32[]{:S(2)}) copy-start(bf16[8,16,768]{2,1,0:T(8,128)(2,1)} %param.45) | copy-start | bytes 589828
  2089.5 3.4 copy-start.12
  2092.9 2.5 copy-start.11
  2095.4 2.5 copy-start.10
  2097.9 10.7 slice-start.2
  2099.3 9.3 slice-start.3
  2099.3 9.3 slice-start.4
Sparse Core Ops, SparseCore 0:
  13.3 199.2 all-gather.4
  214.3 192.2 all-gather.2
  562.9 635.1 reduce-scatter.4
  1200.4 636.2 reduce-scatter.2
  1847.4 242.0 all-reduce.4
where the time goes:
time: 2130 us; the launch traced here: 2120 us
  waiting for transfers between devices  1590 us (75%)
  local copies, waits for them, and re-layouts  146 us (7%)
  blocking collectives  143 us (7%)
  matrix products  137 us (6%)
  starting transfers between devices  51.1 us (2%)
  other arithmetic  29.9 us (1%)
    reduce_scatter x1, waiting for transfers between devices, local(): lax.psum_scatter(grad_keys_all[local_count:], ('gx', 'gy'), scatter_dimen...  633 us
    reduce_scatter x1, waiting for transfers between devices, local(): lax.psum_scatter(grad_values_all[local_count:], ('gx', 'gy'), scatter_dim...  533 us
    all_gather x1, waiting for transfers between devices, local(): lax.all_gather(spaced_values, ('gx', 'gy'), axis=0, tiled=True)  191 us
    psum x1, waiting for transfers between devices, local(): lax.psum((grad_wq, grad_wk, grad_wv, grad_wout, grad_up, grad_down, grad_...  162 us
    unnamed x1, blocking collectives  71.6 us
    psum x1, blocking collectives, local(): lax.psum((grad_wq, grad_wk, grad_wv, grad_wout, grad_up, grad_down, grad_...  71.1 us
    all_gather x1, waiting for transfers between devices, local(): lax.all_gather(spaced_keys, ('gx', 'gy'), axis=0, tiled=True)  54.4 us
    dot_general x18, matrix products, product(): return jnp.dot(left_op, right_op, preferred_element_type=jnp.float32)  43.7 us
  transfers between devices with their start and end apart: 21, of which 8 were waited for; matrix products, arithmetic and copies ran while one was open for 6% of the time, Pallas kernels for 0%

commit v1 on v0

v1 whole, which is shorter than its diff:
```python
import math

import jax
import jax.numpy as jnp
import numpy as np
from jax import lax
from jax.experimental import pallas as pl
from jax.experimental.pallas import tpu as pltpu
from jax.sharding import PartitionSpec as P

HEADS = 16
HEAD_DIM = 48
SLOT = 64
PAIRS = HEADS // 2
STRIDE = 4
WINDOW = 8
ROWS = 8
COLS = 16
TOKENS = ROWS * COLS
N_GX = 32
N_GY = 4
N_DEV = N_GX * N_GY
AXES = ("gx", "gy")
BF = jnp.bfloat16
F32 = jnp.float32
SCALE = 1.0 / math.sqrt(HEAD_DIM)
SCALE_LOG2 = SCALE * math.log2(math.e)
MARK = 1e30
HIDE = -1e30
CHUNK = 128
epsilon = 1e-05

PIECES = ((-1, 0), (1, 0), (0, -1), (0, 1), (-1, -1), (-1, 1), (1, -1), (1, 1))


def nt(left_op, right_op):
    return lax.dot_general(left_op, right_op, (((1,), (1,)), ((), ())), preferred_element_type=F32)


def tn(left_op, right_op):
    return lax.dot_general(left_op, right_op, (((0,), (0,)), ((), ())), preferred_element_type=F32)


def product(left_op, right_op):
    return jnp.dot(left_op, right_op, preferred_element_type=F32)


def coords(flat):
    core, x_hi, z, x_lo, y = flat & 1, (flat >> 1) & 1, (flat >> 2) & 3, (flat >> 4) & 1, flat >> 5
    return (x_hi * 2 + x_lo, y, z, core)


def flat_of(place):
    x, y, z, core = place
    return y * 32 + (x & 1) * 16 + z * 4 + (x >> 1) * 2 + core


def core_pairs():
    return [(i, i ^ 1) for i in range(N_DEV)]


def ring_pairs(order, stage, shift):
    pairs = []
    for i in range(N_DEV):
        place = list(coords(i))
        axis = order[place[3]][stage]
        place[axis] = (place[axis] + shift) % 4
        pairs.append((i, flat_of(place)))
    return pairs


def sent(value, pairs):
    return lax.ppermute(value, AXES, pairs)


def grid_pairs(row_step, col_step):
    pairs = []
    for gx in range(N_GX):
        for gy in range(N_GY):
            sx, sy = gx + col_step, gy + row_step
            if 0 <= sx < N_GX and 0 <= sy < N_GY:
                pairs.append((sx * N_GY + sy, gx * N_GY + gy))
    return pairs


SAME_CORE = [[i for i in range(N_DEV) if i % 2 == core] for core in (0, 1)]
ORDERS = (
    {0: (2, 1, 0), 1: (0, 2, 1)},
    {0: (1, 0, 2), 1: (2, 1, 0)},
    {0: (0, 2, 1), 1: (1, 0, 2)},
)


def total_of(parts):
    total = parts[0].astype(F32)
    for part in parts[1:]:
        total = total + part.astype(F32)
    return total


def all_reduce(array):
    rows, width = array.shape
    third = width // 3
    me = lax.axis_index(AXES)
    x, y, z, core = coords(me)
    place = (x, y, z)
    spots = [
        [jnp.where(core == 0, place[order[0][stage]], place[order[1][stage]]) for stage in range(3)]
        for order in ORDERS
    ]

    def pick(cut, index):
        return lax.dynamic_index_in_dim(cut, index, 0, keepdims=False)

    pieces = []
    for part in range(3):
        order = ORDERS[part]
        held = array[:, part * third : (part + 1) * third].reshape(2, rows // 2, third)
        held = total_of([pick(held, core), sent(pick(held, 1 - core), core_pairs())]).astype(BF)
        for stage in range(3):
            spot = spots[part][stage]
            cut = held.reshape(4, held.shape[0] // 4, third)
            got = [
                sent(pick(cut, (spot + step) % 4), ring_pairs(order, stage, step))
                for step in (2, 1, 3)
            ]
            held = total_of([pick(cut, spot)] + got).astype(BF)
        pieces.append(held)
    for stage in (2, 1, 0):
        for part in range(3):
            order = ORDERS[part]
            spot = spots[part][stage]
            held = pieces[part]
            got = [(step, sent(held, ring_pairs(order, stage, -step))) for step in (2, 1, 3)]
            whole = jnp.zeros((4,) + held.shape, held.dtype)
            for step, piece in [(0, held)] + got:
                whole = lax.dynamic_update_index_in_dim(whole, piece, (spot + step) % 4, 0)
            pieces[part] = whole.reshape(4 * held.shape[0], third)
    outs = []
    for part in range(3):
        held = pieces[part]
        other = sent(held, core_pairs())
        first = jnp.where(core == 0, held, other)
        second = jnp.where(core == 0, other, held)
        outs.append(jnp.concatenate([first, second], axis=0))
    return jnp.concatenate(outs, axis=1)


def gather_far(tokens_far):
    rows, width = tokens_far.shape
    spread = jnp.broadcast_to(tokens_far[None], (N_DEV // 2, rows, width))
    half = lax.all_to_all(spread, AXES, 0, 0, tiled=True, axis_index_groups=SAME_CORE)
    half = half.reshape(N_DEV // 2 * rows, width)
    return jnp.concatenate([half, sent(half, core_pairs())], axis=0)


def scatter_far(grads):
    count, width = grads.shape
    half = count // 2
    mine = total_of([grads[:half], sent(grads[half:], core_pairs())]).astype(BF)
    mine = mine.reshape(N_DEV // 2, half // (N_DEV // 2), width)
    back = lax.all_to_all(mine, AXES, 0, 0, tiled=True, axis_index_groups=SAME_CORE)
    return jnp.sum(back.astype(F32), axis=0)


def halves(block):
    wide = block.astype(F32)
    lane = lax.broadcasted_iota(jnp.int32, wide.shape, 1)
    first = jnp.where(lane < SLOT, wide, 0.0).astype(BF)
    second = jnp.where(lane < SLOT, 0.0, wide).astype(BF)
    return jnp.concatenate([first, second], axis=0)


def own_blocks(wide):
    row = lax.broadcasted_iota(jnp.int32, (2 * SLOT, TOKENS), 0)
    return jnp.where(row < SLOT, wide[:, :TOKENS], wide[:, TOKENS:]).T


def folded(tile, op):
    return op(tile.reshape(tile.shape[0] // 8, 8, tile.shape[1]), axis=0)


def attend_kernel(q_ref, k_ref, vt_ref, bias_ref, o_ref, lse_ref, t_ref, e_ref):
    keys = k_ref.shape[0]
    query_rows = halves(q_ref[...])
    top = jnp.full((8, 2 * TOKENS), HIDE, F32)
    for start in range(0, keys, CHUNK):
        rows = pl.ds(start, CHUNK)
        bias = bias_ref[rows, :]
        tile = nt(k_ref[rows, :], query_rows) * SCALE_LOG2 + jnp.concatenate([bias, bias], axis=1)
        t_ref[rows, :] = tile
        top = jnp.maximum(top, folded(tile, jnp.max))
    top = jnp.max(top, axis=0, keepdims=True)
    total = jnp.zeros((8, 2 * TOKENS), F32)
    for start in range(0, keys, CHUNK):
        rows = pl.ds(start, CHUNK)
        tile = jnp.exp2(t_ref[rows, :] - top)
        total = total + folded(tile, jnp.sum)
        e_ref[rows, :] = tile.astype(BF)
    total = jnp.sum(total, axis=0, keepdims=True)
    wide = jnp.dot(vt_ref[...], e_ref[...], preferred_element_type=F32) / total
    o_ref[...] = own_blocks(wide)
    lse_ref[0] = top + jnp.log2(total)


def attend_back_kernel(
    q_ref, g_ref, o_ref, k_ref, v_ref, kt_ref, bias_ref, lse_ref, gq_ref, gk_ref, gv_ref, s_ref
):
    keys = k_ref.shape[0]
    query_rows = halves(q_ref[...])
    grad_rows = halves(g_ref[...])
    inner = (g_ref[...].astype(F32) * o_ref[...]).T
    inner = jnp.concatenate(
        [
            jnp.sum(inner[:SLOT], axis=0, keepdims=True),
            jnp.sum(inner[SLOT:], axis=0, keepdims=True),
        ],
        axis=1,
    )
    lse = lse_ref[0]
    for start in range(0, keys, CHUNK):
        rows = pl.ds(start, CHUNK)
        bias = bias_ref[rows, :]
        tile = nt(k_ref[rows, :], query_rows) * SCALE_LOG2 + jnp.concatenate([bias, bias], axis=1)
        probs = jnp.exp2(tile - lse)
        grad_probs = nt(v_ref[rows, :], grad_rows)
        grad_scores = (probs * (grad_probs - inner)).astype(BF)
        s_ref[rows, :] = grad_scores
        gv_ref[rows, :] = jnp.dot(
            probs.astype(BF), grad_rows, preferred_element_type=F32
        ).astype(BF)
        gk_ref[rows, :] = (
            jnp.dot(grad_scores, query_rows, preferred_element_type=F32) * SCALE
        ).astype(BF)
    wide = jnp.dot(kt_ref[...], s_ref[...], preferred_element_type=F32) * SCALE
    gq_ref[...] = own_blocks(wide).astype(BF)


def rows_spec(count):
    return pl.BlockSpec((count, 2 * SLOT), lambda p: (0, p))


def cols_spec(count):
    return pl.BlockSpec((2 * SLOT, count), lambda p: (p, 0))


def attend(queries, keys, values_t, bias):
    count = keys.shape[0]
    return pl.pallas_call(
        attend_kernel,
        grid=(PAIRS,),
        in_specs=[
            rows_spec(TOKENS),
            rows_spec(count),
            cols_spec(count),
            pl.BlockSpec((count, TOKENS), lambda p: (0, 0)),
        ],
        out_specs=[rows_spec(TOKENS), pl.BlockSpec((1, 1, 2 * TOKENS), lambda p: (p, 0, 0))],
        out_shape=[
            jax.ShapeDtypeStruct((TOKENS, HEADS * SLOT), F32),
            jax.ShapeDtypeStruct((PAIRS, 1, 2 * TOKENS), F32),
        ],
        scratch_shapes=[
            pltpu.VMEM((count, 2 * TOKENS), F32),
            pltpu.VMEM((count, 2 * TOKENS), BF),
        ],
        compiler_params=pltpu.CompilerParams(vmem_limit_bytes=32 * 1024 * 1024),
        cost_estimate=pl.CostEstimate(
            flops=4 * PAIRS * count * 256 * 128,
            bytes_accessed=6 * count * HEADS * SLOT,
            transcendentals=HEADS * count * TOKENS,
        ),
        name="attend",
    )(queries, keys, values_t, bias)


def attend_back(queries, grads, outs, keys, values, keys_t, bias, lse):
    count = keys.shape[0]
    return pl.pallas_call(
        attend_back_kernel,
        grid=(PAIRS,),
        in_specs=[
            rows_spec(TOKENS),
            rows_spec(TOKENS),
            rows_spec(TOKENS),
            rows_spec(count),
            rows_spec(count),
            cols_spec(count),
            pl.BlockSpec((count, TOKENS), lambda p: (0, 0)),
            pl.BlockSpec((1, 1, 2 * TOKENS), lambda p: (p, 0, 0)),
        ],
        out_specs=[rows_spec(TOKENS), rows_spec(count), rows_spec(count)],
        out_shape=[
            jax.ShapeDtypeStruct((TOKENS, HEADS * SLOT), BF),
            jax.ShapeDtypeStruct((count, HEADS * SLOT), BF),
            jax.ShapeDtypeStruct((count, HEADS * SLOT), BF),
        ],
        scratch_shapes=[pltpu.VMEM((count, 2 * TOKENS), BF)],
        compiler_params=pltpu.CompilerParams(vmem_limit_bytes=32 * 1024 * 1024),
        cost_estimate=pl.CostEstimate(
            flops=10 * PAIRS * count * 256 * 128,
            bytes_accessed=10 * count * HEADS * SLOT,
            transcendentals=HEADS * count * TOKENS,
        ),
        name="attend_back",
    )(queries, grads, outs, keys, values, keys_t, bias, lse)


def layer_norm(inputs, gain_vec, shift_vec):
    row_mean = jnp.mean(inputs, axis=-1, keepdims=True)
    centered = inputs - row_mean
    row_var = jnp.mean(centered * centered, axis=-1, keepdims=True)
    return centered * lax.rsqrt(row_var + epsilon) * gain_vec + shift_vec


def exact_gelu(inputs):
    return jax.nn.gelu(inputs, approximate=False)


def padded_cols(weight):
    width = weight.shape[0]
    cut = weight.reshape(width, HEADS, HEAD_DIM)
    return jnp.pad(cut, ((0, 0), (0, 0), (0, SLOT - HEAD_DIM))).reshape(width, HEADS * SLOT)


def padded_rows(weight):
    width = weight.shape[1]
    cut = weight.reshape(HEADS, HEAD_DIM, width)
    return jnp.pad(cut, ((0, 0), (0, SLOT - HEAD_DIM), (0, 0))).reshape(HEADS * SLOT, width)


def real_rows(weight):
    width = weight.shape[1]
    return weight.reshape(HEADS, SLOT, width)[:, :HEAD_DIM].reshape(HEADS * HEAD_DIM, width)


def piece_of(block, row_step, col_step):
    if col_step == 0:
        return block
    return block[:, WINDOW:] if col_step < 0 else block[:, : COLS - WINDOW]


def window_weights():
    rows, cols = np.mgrid[0:ROWS, 0:COLS]
    query = (rows.reshape(-1), cols.reshape(-1))
    key_rows, key_cols = [rows.reshape(-1)], [cols.reshape(-1)]
    for row_step, col_step in PIECES:
        key_rows.append(piece_of(rows, row_step, col_step).reshape(-1) + row_step * ROWS)
        key_cols.append(piece_of(cols, row_step, col_step).reshape(-1) + col_step * COLS)
    row_gap = np.concatenate(key_rows)[:, None] - query[0][None]
    col_gap = np.concatenate(key_cols)[:, None] - query[1][None]
    dense = (np.abs(row_gap) <= WINDOW) & (np.abs(col_gap) <= WINDOW)
    dilated = dense & (row_gap % 2 == 0) & (col_gap % 2 == 0)
    itself = (row_gap == 0) & (col_gap == 0)
    return np.where(dense, np.where(dilated, 1.0, 0.0), HIDE).astype(np.float32), itself


def local(
    embeddings,
    tile_valid,
    w_query,
    w_key,
    w_value,
    w_out,
    w_up,
    w_down,
    gain_attn,
    shift_attn,
    gain_mlp,
    shift_mlp,
    cotangent,
):
    width = embeddings.shape[-1]
    gx, gy = lax.axis_index("gx"), lax.axis_index("gy")
    residual = embeddings.astype(F32).reshape(TOKENS, width)
    normed_attn, attn_norm_back = jax.vjp(layer_norm, residual, gain_attn, shift_attn)
    act_attn = normed_attn.astype(BF)

    own_flags = tile_valid.reshape(TOKENS, 1) > 0
    marked = jnp.where(own_flags, act_attn, jnp.asarray(MARK, BF)).reshape(ROWS, COLS, width)
    far_got = gather_far(marked[::STRIDE, ::STRIDE].reshape(-1, width))
    pieces = []
    exists = [jnp.ones((TOKENS,), jnp.bool_)]
    for row_step, col_step in PIECES:
        piece = sent(piece_of(marked, row_step, col_step), grid_pairs(row_step, col_step))
        piece = piece.reshape(-1, width)
        there = (
            (gy + row_step >= 0)
            & (gy + row_step < N_GY)
            & (gx + col_step >= 0)
            & (gx + col_step < N_GX)
        )
        exists.append(jnp.broadcast_to(there, (piece.shape[0],)))
        pieces.append(piece)
    near_got = jnp.concatenate(pieces, axis=0)
    limit = jnp.asarray(MARK / 2, BF)
    got = jnp.concatenate([near_got, far_got], axis=0)
    got_valid = got[:, :1] < limit
    act_all = jnp.concatenate([act_attn, jnp.where(got < limit, got, jnp.zeros_like(got))], axis=0)
    near_count = TOKENS + near_got.shape[0]
    far_count = far_got.shape[0]

    flags = jnp.concatenate([own_flags, got_valid], axis=0)
    flags = flags & jnp.concatenate(exists + [jnp.ones((far_count,), jnp.bool_)])[:, None]
    log_weight, itself = window_weights()
    near_bias = jnp.where(flags[:near_count] | itself, log_weight, HIDE)
    far_bias = jnp.broadcast_to(jnp.where(flags[near_count:], 0.0, HIDE), (far_count, TOKENS))
    bias = jnp.concatenate([near_bias, far_bias], axis=0).astype(F32)

    wq, wk, wv = padded_cols(w_query), padded_cols(w_key), padded_cols(w_value)
    wo = padded_rows(w_out)
    queries = product(act_attn, wq).astype(BF)
    keys = product(act_all, wk).astype(BF)
    values = product(act_all, wv).astype(BF)
    keys_t, values_t = keys.T, values.T

    outs, lse = attend(queries, keys, values_t, bias)
    attended = outs.astype(BF)
    middle = residual + product(attended, wo)
    normed_mlp, mlp_norm_back = jax.vjp(layer_norm, middle, gain_mlp, shift_mlp)
    act_mlp = normed_mlp.astype(BF)
    pre_act = product(act_mlp, w_up)
    gelu_out, gelu_back = jax.vjp(exact_gelu, pre_act)
    hidden = gelu_out.astype(BF)
    output = middle + product(hidden, w_down)

    grad_out = cotangent.reshape(TOKENS, width)
    grad_down = tn(hidden, grad_out)
    grad_pre = gelu_back(nt(grad_out, w_down))[0].astype(BF)
    grad_up = tn(act_mlp, grad_pre)
    grad_up, grad_down = lax.psum((grad_up.astype(BF), grad_down.astype(BF)), AXES)

    grad_act_mlp = nt(grad_pre, w_up)
    grad_mid_norm, grad_gain_mlp, grad_shift_mlp = mlp_norm_back(grad_act_mlp)
    grad_mid = grad_out.astype(F32) + grad_mid_norm
    grad_branch = grad_mid.astype(BF)
    grad_wout = tn(attended, grad_branch)
    grad_att = nt(grad_branch, wo).astype(BF)

    grad_query, grad_keys, grad_values = attend_back(
        queries, grad_att, outs, keys, values, keys_t, bias, lse
    )
    grad_act_all = nt(grad_keys, wk) + nt(grad_values, wv)
    far_back = scatter_far(grad_act_all[near_count:].astype(BF))
    near_back = grad_act_all[TOKENS:near_count].astype(BF)

    grad_act = nt(grad_query, wq) + grad_act_all[:TOKENS]
    grad_act = grad_act.reshape(ROWS, COLS, width)
    grad_act = grad_act + lax.pad(
        far_back.reshape(ROWS // STRIDE, COLS // STRIDE, width),
        jnp.zeros((), F32),
        ((0, STRIDE - 1, STRIDE - 1), (0, STRIDE - 1, STRIDE - 1), (0, 0, 0)),
    )
    sides = {-1: jnp.zeros((ROWS, WINDOW, width), F32), 1: jnp.zeros((ROWS, WINDOW, width), F32)}
    start = 0
    for row_step, col_step in PIECES:
        count = TOKENS if col_step == 0 else TOKENS // 2
        back = sent(near_back[start : start + count], grid_pairs(-row_step, -col_step))
        start += count
        if col_step == 0:
            grad_act = grad_act + back.astype(F32).reshape(ROWS, COLS, width)
        else:
            sides[col_step] = sides[col_step] + back.astype(F32).reshape(ROWS, WINDOW, width)
    grad_act = grad_act + jnp.concatenate([sides[1], sides[-1]], axis=1)
    grad_in_norm, grad_gain_attn, grad_shift_attn = attn_norm_back(grad_act.reshape(TOKENS, width))
    grad_inputs = grad_mid + grad_in_norm

    small = jnp.stack([grad_gain_attn, grad_shift_attn, grad_gain_mlp, grad_shift_mlp])
    small = lax.psum(small, AXES)
    stacked = jnp.concatenate(
        [
            grad_wout_rows.astype(BF)
            for grad_wout_rows in (
                real_rows(grad_wout),
                real_rows(tn(grad_query, act_attn)),
                real_rows(tn(grad_keys, act_all)),
                real_rows(tn(grad_values, act_all)),
            )
        ],
        axis=0,
    )
    summed = all_reduce(stacked).astype(F32).reshape(4, width, width)
    mixed = output.astype(BF).reshape(ROWS, COLS, width)
    return (
        mixed,
        grad_inputs.reshape(ROWS, COLS, width),
        summed[1].T,
        summed[2].T,
        summed[3].T,
        summed[0],
        grad_up.astype(F32),
        grad_down.astype(F32),
        small[0],
        small[1],
        small[2],
        small[3],
    )


def solution(mesh):
    grid = P("gy", "gx", None)
    in_specs = (grid, P("gy", "gx")) + (P(),) * 10 + (grid,)
    out_specs = (grid, grid) + (P(),) * 10
    return jax.shard_map(local, mesh=mesh, in_specs=in_specs, out_specs=out_specs, check_vma=False)
```

time: 2130 us -> 544 us (0.26)
  waiting for transfers between devices: 1590 us -> 34.4 us
  starting transfers between devices: 51.1 us -> 157 us
  matrix products: 137 us -> 57.8 us
  local copies, waits for them, and re-layouts: 146 us -> 88.4 us
  blocking collectives: 143 us -> 90.6 us
  Pallas kernels: 0 us -> 38.8 us
  other arithmetic: 29.9 us -> 55.5 us
    reduce_scatter x2 -> x0, waiting for transfers between devices: 1170 us -> none  [the longest x1 633 us: local(): lax.psum_scatter(grad_keys_all[local_count:], ('gx', 'gy'), scatter_dimen...]
    all_gather x2 -> x0, waiting for transfers between devices: 246 us -> none  [the longest x1 191 us: local(): lax.all_gather(spaced_values, ('gx', 'gy'), axis=0, tiled=True)]
    psum x1, waiting for transfers between devices: 162 us -> 0.01 us  [local(): lax.psum((grad_up.astype(BF), grad_down.astype(BF)), AXES)]
    ppermute x16 -> x78, starting transfers between devices: 50.9 us -> 144 us  [sent(): return lax.ppermute(value, AXES, pairs)]
    dot_general x74 -> x18, matrix products: 137 us -> 57.8 us  [the longest x6 20.8 us: nt(): lax.dot_general(left_op, right_op, (((1,), (1,)), ((), ())), preferred_el...]
    unnamed x1 -> x0, blocking collectives: 71.6 us -> none
    pallas_call x0 -> x2, Pallas kernels: none -> 38.8 us  [the longest x1 28.1 us: attend_back(): pl.pallas_call(attend_back_kernel, grid=(PAIRS,), in_specs=[rows_spec(TOK...]
    slice x18 -> x13, local copies, waits for them, and re-layouts: 43.5 us -> 11.3 us  [the longest x1 3.11 us: local(): summed[0]]
  transfers between devices with their start and end apart: 21 -> 80, of which waited for: 8 -> 23; matrix products, arithmetic and copies ran while one was open for 6% -> 18% of each run, Pallas kernels for 0% -> 0%
where the time goes in v1:
time: 544 us; the launch traced here: 539 us
  starting transfers between devices  157 us (29%)
  blocking collectives  90.6 us (17%)
  local copies, waits for them, and re-layouts  88.4 us (16%)
  matrix products  57.8 us (11%)
  other arithmetic  55.5 us (10%)
  Pallas kernels  38.8 us (7%)
  waiting for transfers between devices  34.4 us (6%)
  between operations  15.8 us (3%)
    ppermute x78, starting transfers between devices, sent(): return lax.ppermute(value, AXES, pairs)  144 us
    psum x1, blocking collectives, local(): small = lax.psum(small, AXES)  64.8 us
    ppermute x78, waiting for transfers between devices, sent(): return lax.ppermute(value, AXES, pairs)  34.4 us
    pallas_call x1, Pallas kernels, attend_back(): pl.pallas_call(attend_back_kernel, grid=(PAIRS,), in_specs=[rows_spec(TOK...  28.1 us
    all_to_all x1, blocking collectives, gather_far(): lax.all_to_all(spread, AXES, 0, 0, tiled=True, axis_index_groups=SAME_CORE)  25.8 us
    unnamed x112, local copies, waits for them, and re-layouts  25.7 us
    dot_general x6, matrix products, nt(): lax.dot_general(left_op, right_op, (((1,), (1,)), ((), ())), preferred_el...  20.8 us
    convert_element_type x1, other arithmetic, local(): summed = all_reduce(stacked).astype(F32).reshape(4, width, width)  20.1 us
  transfers between devices with their start and end apart: 80, of which 23 were waited for; matrix products, arithmetic and copies ran while one was open for 18% of the time, Pallas kernels for 0%

profile of v1, /device:TPU:1, one launch (start us, length us, event | category | flops | bytes accessed | tf_op | source)
XLA Modules:
  0.0 538.6 jit_solution(3257208164141142039)
XLA Ops:
  11.5 25.8 %all_to_all.10 = bf16[64,8,768]{2,1,0:T(8,128)(2,1)S(1)} all-to-all(bf16[64,8,768]{2,1,0:T(8,128)(2,1)S(1)} %broadcast_in_dim.208), channel_id=1, replica_groups={{0,2,4,6,8,10,12,14,16,18,20,22,24,26,28,30,32,34,36,38,40,42,44,46,48,..., dimensions={0} | all-to-all | bytes 1572864 | tf_op jit(solution)/shard_map/all_to_all | solution.py:152
  38.4 2.8 collective-permute-start.8
  41.8 3.0 collective-permute-start.2
  44.9 3.2 collective-permute-start.4
  53.6 2.4 collective-permute-start
  56.1 2.7 collective-permute-start.1
  58.7 4.5 collective-permute-start.6
  70.0 2.6 pad.20
  89.2 4.0 concatenate.50
  95.1 4.4 convolution_convert_fusion.2
  99.5 6.1 %copy.127.k_ref = bf16[1792,1024]{1,0:T(8,128)(2,1)} copy(bf16[1792,1024]{0,1:T(8,128)(2,1)} %convolution_convert_fusion.2) | data formatting | bytes 7340032 | tf_op jit(solution)/shard_map/convert_element_type | solution.py:413
  105.6 6.4 %convolution_convert_fusion.3.v_ref = bf16[1792,1024]{1,0:T(8,128)(2,1)} fusion(bf16[768,1024]{0,1:T(8,128)(2,1)} %bitcast.333, bf16[1664,768]{0,1:T(8,128)(2,1)S(1)} %copy-done.21, bf16[128,768]{0,1:T(8,128)(2,1)} %add_convert_fusion.3), kind=kOutput, calls=%fused_computation.6 | convolution fusion | flops 2825912320 | bytes 7995392 | tf_op jit(solution)/shard_map/dot_general | solution.py:45
  112.0 6.0 %copy.128.vt_ref = bf16[1024,1792]{1,0:T(8,128)(2,1)} copy(bf16[1024,1792]{0,1:T(8,128)(2,1)} %bitcast.294) | data formatting | bytes 7340032 | tf_op jit(solution)/shard_map/convert_element_type | solution.py:414
  118.5 2.0 copy-done
  120.5 2.0 copy-done.2
  122.6 10.7 %attend.1 = (f32[128,1024]{1,0:T(8,128)S(1)}, f32[8,1,256]{2,1,0:T(1,128)S(1)}) custom-call(bf16[128,1024]{1,0:T(8,128)(2,1)S(1)} %convolution_convert_fusion.8.q_ref, bf16[1792,1024]{1,0:T(8,128)(2,1)S(1)} %copy-done, bf16[1024,1792]{1,0:T(8,128)(2,1)S(1)} %copy-done.2, f32[1792,128]{1,0:T(8,128)S(1)} %pad_maximum_fusion.2.bias_ref), custom_call_target="tpu_custom_call" | custom-call | flops 1879048192 | bytes 11010048 | tf_op jit(solution)/shard_map/attend/pallas_call | solution.py:249
  134.2 3.4 fusion.58
  137.7 6.1 %add_convert_fusion.1 = (bf16[128,3072]{1,0:T(8,128)(2,1)S(1)}, f32[128,3072]{1,0:T(8,128)}) fusion(f32[128,3072]{1,0:T(8,128)S(1)} %fusion.58, bf16[128,768]{1,0:T(8,128)(2,1)S(1)} %bitcast.361, bf16[3072,768]{1,0:T(8,128)(2,1)S(1)} %bitcast.315), kind=kOutput, calls=%fused_computation.26 | convolution fusion | flops 632291328 | bytes 8847360 | tf_op jit(solution)/shard_map/dot_general | solution.py:37
  143.9 2.4 fusion.71
  148.1 2.4 convolution_convert_fusion.7.g_ref
  150.5 2.0 copy-done.3
  152.6 2.0 copy-done.4
  154.6 28.1 %attend_back.1 = (bf16[128,1024]{1,0:T(8,128)(2,1)S(1)}, bf16[1792,1024]{1,0:T(8,128)(2,1)S(1)}, bf16[1792,1024]{1,0:T(8,128)(2,1)S(1)}) custom-call(bf16[128,1024]{1,0:T(8,128)(2,1)S(1)} %convolution_convert_fusion.8.q_ref, bf16[128,1024]{1,0:T(8,128)(2,1)S(1)} %convolution_convert_fusion.7.g_ref, f32[128,1024]{1,0:T(8,128)S(1)} %get-tuple-element.17.o_ref, ...), custom_call_target="tpu_custom_call" | custom-call | flops 4697620480 | bytes 18350080 | tf_op jit(solution)/shard_map/attend_back/pallas_call | solution.py:279
  182.8 3.0 fusion.72
  185.8 4.7 fusion.70
  193.7 4.2 convolution_convert_fusion.5
  197.9 4.4 convolution_convert_fusion.6
  204.1 3.7 convolution_convert_fusion.1
  207.9 2.3 fusion.9
  210.2 3.6 convolution_convert_fusion
  220.9 2.2 convolution_add_fusion.2
  234.6 9.4 %collective-permute-start.14 = (bf16[64,768]{1,0:T(8,128)(2,1)S(1)}, bf16[64,768]{1,0:T(8,128)(2,1)S(1)}, u32[]{:S(2)}, u32[]{:S(2)}) collective-permute-start(bf16[64,768]{1,0:T(8,128)(2,1)S(1)} %copy-done.44), channel_id=1, source_target_pairs={{0,5},{1,6},{2,7},{4,9},{5,10},{6,11},{8,13},{9,14},{10,15},{12,17... | collective-permute-start | bytes 294920 | tf_op jit(solution)/shard_map/ppermute | solution.py:73
  244.0 3.4 collective-permute-start.13
  247.4 3.9 collective-permute-start.12
  252.4 7.0 %collective-permute-start.11 = (bf16[128,768]{1,0:T(8,128)(2,1)}, bf16[128,768]{1,0:T(8,128)(2,1)}, u32[]{:S(2)}, u32[]{:S(2)}) collective-permute-start(bf16[128,768]{1,0:T(8,128)(2,1)} %get-tuple-element.127), channel_id=1, source_target_pairs={{0,1},{1,2},{2,3},{4,5},{5,6},{6,7},{8,9},{9,10},{10,11},{12,13},{... | collective-permute-start | bytes 589832 | tf_op jit(solution)/shard_map/ppermute | solution.py:73
  262.7 2.4 fusion.10
  265.1 13.3 %all-to-all-start.1 = ((bf16[64,8,768]{2,1,0:T(8,128)(2,1)}), bf16[64,8,768]{2,1,0:T(8,128)(2,1)}, u32[]{:S(2)}, u32[]{:S(2)}) async-start(bf16[64,8,768]{2,1,0:T(8,128)(2,1)} %fusion.10), calls=%async_computation.1 | async-start | bytes 1572864 | tf_op jit(solution)/shard_map/all_to_all | solution.py:162
  280.0 2.6 collective-permute-start.61
  287.2 6.9 %collective-permute-done.61 = bf16[384,256]{1,0:T(8,128)(2,1)S(1)} collective-permute-done((bf16[384,256]{1,0:T(8,128)(2,1)S(1)}, bf16[384,256]{1,0:T(8,128)(2,1)S(1)}, u32[]{:S(2)}, u32[]{:S(2)}) %collective-permute-start.61) | collective-permute-done | bytes 196640 | tf_op jit(solution)/shard_map/ppermute | solution.py:73
  295.6 2.1 collective-permute-start.40
  299.4 2.8 collective-permute-start.21
  302.3 4.0 collective-permute-start.20
  306.5 2.9 collective-permute-start.64
  309.9 2.2 collective-permute-start.63
  313.4 2.7 collective-permute-start.62
  316.2 2.8 collective-permute-start.44
  319.1 5.3 collective-permute-start.42
  333.5 2.0 collective-permute-start.46
  339.6 2.0 collective-permute-start.25
  348.2 2.1 collective-permute-done.48
  372.5 2.1 collective-permute-done.74
  375.5 2.3 collective-permute-start.55
  378.0 3.5 collective-permute-done.54
  385.7 3.8 collective-permute-done.34
  389.6 16.1 %collective-permute-start.77 = (bf16[1536,256]{1,0:T(8,128)(2,1)S(1)}, bf16[1536,256]{1,0:T(8,128)(2,1)}, u32[]{:S(2)}, u32[]{:S(2)}) collective-permute-start(bf16[1536,256]{1,0:T(8,128)(2,1)S(1)} %bitcast.330), channel_id=1, source_target_pairs={{0,1},{1,0},{2,3},{3,2},{4,5},{5,4},{6,7},{7,6},{8,9},{9,8},{10,11... | collective-permute-start | bytes 2359304 | tf_op jit(solution)/shard_map/ppermute | solution.py:73
  405.6 4.2 collective-permute-start.57
  409.9 2.8 collective-permute-start.37
  418.9 64.8 %psum.23 = f32[4,768]{1,0:T(4,128)S(1)} all-reduce(f32[4,768]{1,0:T(4,128)S(1)} %pad_maximum_fusion.3), channel_id=1, replica_groups=mesh['gx'=32,'gy'=4] {'gx','gy'}, use_global_device_ids=true, to_apply=%region_15.16 | all-reduce | flops 3072 | bytes 24576 | tf_op jit(solution)/shard_map/psum | solution.py:469
  488.3 20.1 %maximum_convert_fusion = f32[3072,768]{1,0:T(8,128)S(1)} fusion(bf16[1536,256]{1,0:T(8,128)(2,1)S(1)} %get-tuple-element.139, bf16[1536,256]{1,0:T(8,128)(2,1)S(1)} %get-tuple-element.138, bf16[1536,256]{1,0:T(8,128)(2,1)S(1)} %get-tuple-element.137, bf16[1536,256]{1,0:T(8,128)(2,1)S(1)} %get-tuple-element.136, bf16[1536,256]{1,0:T(8,128)(2,1)S(1)} %get-tuple-element.135, ...), kind=kLoop, calls=%fused_computation.4 | loop fusion | flops 28311552 | bytes 14155776 | tf_op jit(solution)/shard_map/convert_element_type | solution.py:482
  508.4 3.1 fusion.64
  511.5 3.0 copy.140
  514.5 3.0 copy.141
  519.5 7.5 %convert_element_type.418 = f32[768,3072]{1,0:T(8,128)} convert(bf16[768,3072]{1,0:T(8,128)(2,1)} %get-tuple-element.103) | non-fusion elementwise | flops 2359296 | bytes 14155776 | tf_op jit(solution)/shard_map/convert_element_type | solution.py:491
  527.0 4.5 convert_element_type.420
  (402 shorter events, 138.8 us)
Async XLA Ops:
  7.2 512.3 %all-reduce.8.cloned.1.call-start = ((), (), s32[]{:S(2)}) async-start(), calls=%async_computation.2 | async-start | bytes 18874368 | tf_op jit(solution)/shard_map/psum | solution.py:431
  38.4 50.8 %collective-permute-start.8 = (bf16[512,768]{0,1:T(8,128)(2,1)}, bf16[512,768]{0,1:T(8,128)(2,1)}, u32[]{:S(2)}, u32[]{:S(2)}) collective-permute-start(bf16[512,768]{0,1:T(8,128)(2,1)} %copy.123), channel_id=1, source_target_pairs={{0,1},{1,0},{2,3},{3,2},{4,5},{5,4},{6,7},{7,6},{8,9},{9,8},{10,11... | collective-permute-start | bytes 2359304 | tf_op jit(solution)/shard_map/ppermute | solution.py:73
  41.8 11.8 %collective-permute-start.2 = (bf16[8,8,768]{2,1,0:T(8,128)(2,1)}, bf16[8,8,768]{2,1,0:T(8,128)(2,1)}, u32[]{:S(2)}, u32[]{:S(2)}) collective-permute-start(bf16[8,8,768]{2,1,0:T(8,128)(2,1)} %get-tuple-element.159), channel_id=1, source_target_pairs={{0,4},{1,5},{2,6},{3,7},{4,8},{5,9},{6,10},{7,11},{8,12},{9,13},{1... | collective-permute-start | bytes 294920 | tf_op jit(solution)/shard_map/ppermute | solution.py:73
  44.9 13.9 %collective-permute-start.4 = (bf16[8,8,768]{2,1,0:T(8,128)(2,1)}, bf16[8,8,768]{2,1,0:T(8,128)(2,1)}, u32[]{:S(2)}, u32[]{:S(2)}) collective-permute-start(bf16[8,8,768]{2,1,0:T(8,128)(2,1)} %get-tuple-element.159), channel_id=1, source_target_pairs={{0,5},{1,6},{2,7},{4,9},{5,10},{6,11},{8,13},{9,14},{10,15},{12,17... | collective-permute-start | bytes 294920 | tf_op jit(solution)/shard_map/ppermute | solution.py:73
  48.1 8.0 %collective-permute-start.3 = (bf16[8,8,768]{2,1,0:T(8,128)(2,1)S(1)}, bf16[8,8,768]{2,1,0:T(8,128)(2,1)}, u32[]{:S(2)}, u32[]{:S(2)}) collective-permute-start(bf16[8,8,768]{2,1,0:T(8,128)(2,1)S(1)} %get-tuple-element.158), channel_id=1, source_target_pairs={{4,0},{5,1},{6,2},{7,3},{8,4},{9,5},{10,6},{11,7},{12,8},{13,9},{1... | collective-permute-start | bytes 294920 | tf_op jit(solution)/shard_map/ppermute | solution.py:73
  49.4 13.9 %collective-permute-start.5 = (bf16[8,8,768]{2,1,0:T(8,128)(2,1)S(1)}, bf16[8,8,768]{2,1,0:T(8,128)(2,1)}, u32[]{:S(2)}, u32[]{:S(2)}) collective-permute-start(bf16[8,8,768]{2,1,0:T(8,128)(2,1)S(1)} %get-tuple-element.158), channel_id=1, source_target_pairs={{4,1},{5,2},{6,3},{8,5},{9,6},{10,7},{12,9},{13,10},{14,11},{16,13... | collective-permute-start | bytes 294920 | tf_op jit(solution)/shard_map/ppermute | solution.py:73
  53.6 32.1 %collective-permute-start = (bf16[8,16,768]{2,1,0:T(8,128)(2,1)S(1)}, bf16[8,16,768]{2,1,0:T(8,128)(2,1)}, u32[]{:S(2)}, u32[]{:S(2)}) collective-permute-start(bf16[8,16,768]{2,1,0:T(8,128)(2,1)S(1)} %get-tuple-element.117), channel_id=1, source_target_pairs={{0,1},{1,2},{2,3},{4,5},{5,6},{6,7},{8,9},{9,10},{10,11},{12,13},{... | collective-permute-start | bytes 589832 | tf_op jit(solution)/shard_map/ppermute | solution.py:73
  56.1 31.4 %collective-permute-start.1 = (bf16[8,16,768]{2,1,0:T(8,128)(2,1)S(1)}, bf16[8,16,768]{2,1,0:T(8,128)(2,1)}, u32[]{:S(2)}, u32[]{:S(2)}) collective-permute-start(bf16[8,16,768]{2,1,0:T(8,128)(2,1)S(1)} %get-tuple-element.117), channel_id=1, source_target_pairs={{1,0},{2,1},{3,2},{5,4},{6,5},{7,6},{9,8},{10,9},{11,10},{13,12},{... | collective-permute-start | bytes 589832 | tf_op jit(solution)/shard_map/ppermute | solution.py:73
  58.7 23.5 %collective-permute-start.6 = (bf16[8,8,768]{2,1,0:T(8,128)(2,1)}, bf16[8,8,768]{2,1,0:T(8,128)(2,1)}, u32[]{:S(2)}, u32[]{:S(2)}) collective-permute-start(bf16[8,8,768]{2,1,0:T(8,128)(2,1)} %get-tuple-element.159), channel_id=1, source_target_pairs={{1,4},{2,5},{3,6},{5,8},{6,9},{7,10},{9,12},{10,13},{11,14},{13,16... | collective-permute-start | bytes 294920 | tf_op jit(solution)/shard_map/ppermute | solution.py:73
  63.3 20.7 %collective-permute-start.7 = (bf16[8,8,768]{2,1,0:T(8,128)(2,1)S(1)}, bf16[8,8,768]{2,1,0:T(8,128)(2,1)}, u32[]{:S(2)}, u32[]{:S(2)}) collective-permute-start(bf16[8,8,768]{2,1,0:T(8,128)(2,1)S(1)} %get-tuple-element.158), channel_id=1, source_target_pairs={{5,0},{6,1},{7,2},{9,4},{10,5},{11,6},{13,8},{14,9},{15,10},{17,12... | collective-permute-start | bytes 294920 | tf_op jit(solution)/shard_map/ppermute | solution.py:73
  213.8 20.0 %collective-permute-start.17 = (bf16[64,768]{1,0:T(8,128)(2,1)}, bf16[64,768]{1,0:T(8,128)(2,1)}, u32[]{:S(2)}, u32[]{:S(2)}) collective-permute-start(bf16[64,768]{1,0:T(8,128)(2,1)} %get-tuple-element.129), channel_id=1, source_target_pairs={{4,1},{5,2},{6,3},{8,5},{9,6},{10,7},{12,9},{13,10},{14,11},{16,13... | collective-permute-start | bytes 294920 | tf_op jit(solution)/shard_map/ppermute | solution.py:73
  215.1 28.9 %collective-permute-start.16 = (bf16[64,768]{1,0:T(8,128)(2,1)}, bf16[64,768]{1,0:T(8,128)(2,1)}, u32[]{:S(2)}, u32[]{:S(2)}) collective-permute-start(bf16[64,768]{1,0:T(8,128)(2,1)} %get-tuple-element.130), channel_id=1, source_target_pairs={{5,0},{6,1},{7,2},{9,4},{10,5},{11,6},{13,8},{14,9},{15,10},{17,12... | collective-permute-start | bytes 294920 | tf_op jit(solution)/shard_map/ppermute | solution.py:73
  216.4 31.0 %collective-permute-start.15 = (bf16[64,768]{1,0:T(8,128)(2,1)}, bf16[64,768]{1,0:T(8,128)(2,1)}, u32[]{:S(2)}, u32[]{:S(2)}) collective-permute-start(bf16[64,768]{1,0:T(8,128)(2,1)} %get-tuple-element.131), channel_id=1, source_target_pairs={{4,0},{5,1},{6,2},{7,3},{8,4},{9,5},{10,6},{11,7},{12,8},{13,9},{1... | collective-permute-start | bytes 294920 | tf_op jit(solution)/shard_map/ppermute | solution.py:73
  217.7 44.5 %collective-permute-start.9 = (bf16[512,768]{1,0:T(8,128)(2,1)}, bf16[512,768]{1,0:T(8,128)(2,1)}, u32[]{:S(2)}, u32[]{:S(2)}) collective-permute-start(bf16[512,768]{1,0:T(8,128)(2,1)} %slice.161), channel_id=1, source_target_pairs={{0,1},{1,0},{2,3},{3,2},{4,5},{5,4},{6,7},{7,6},{8,9},{9,8},{10,11... | collective-permute-start | bytes 2359304 | tf_op jit(solution)/shard_map/ppermute | solution.py:73
  228.8 49.7 %collective-permute-start.58 = (bf16[1536,256]{1,0:T(8,128)(2,1)}, bf16[1536,256]{1,0:T(8,128)(2,1)S(1)}, u32[]{:S(2)}, u32[]{:S(2)}) collective-permute-start(bf16[1536,256]{1,0:T(8,128)(2,1)} %dynamic-slice_bitcast_fusion), channel_id=1, source_target_pairs={{0,1},{1,0},{2,3},{3,2},{4,5},{5,4},{6,7},{7,6},{8,9},{9,8},{10,11... | collective-permute-start | bytes 2359304 | tf_op jit(solution)/shard_map/ppermute | solution.py:73
  234.6 17.7 %collective-permute-start.14 = (bf16[64,768]{1,0:T(8,128)(2,1)S(1)}, bf16[64,768]{1,0:T(8,128)(2,1)S(1)}, u32[]{:S(2)}, u32[]{:S(2)}) collective-permute-start(bf16[64,768]{1,0:T(8,128)(2,1)S(1)} %copy-done.44), channel_id=1, source_target_pairs={{0,5},{1,6},{2,7},{4,9},{5,10},{6,11},{8,13},{9,14},{10,15},{12,17... | collective-permute-start | bytes 294920 | tf_op jit(solution)/shard_map/ppermute | solution.py:73
  244.0 15.4 %collective-permute-start.13 = (bf16[64,768]{1,0:T(8,128)(2,1)S(1)}, bf16[64,768]{1,0:T(8,128)(2,1)S(1)}, u32[]{:S(2)}, u32[]{:S(2)}) collective-permute-start(bf16[64,768]{1,0:T(8,128)(2,1)S(1)} %copy-done.43), channel_id=1, source_target_pairs={{1,4},{2,5},{3,6},{5,8},{6,9},{7,10},{9,12},{10,13},{11,14},{13,16... | collective-permute-start | bytes 294920 | tf_op jit(solution)/shard_map/ppermute | solution.py:73
  247.4 14.0 %collective-permute-start.12 = (bf16[64,768]{1,0:T(8,128)(2,1)S(1)}, bf16[64,768]{1,0:T(8,128)(2,1)S(1)}, u32[]{:S(2)}, u32[]{:S(2)}) collective-permute-start(bf16[64,768]{1,0:T(8,128)(2,1)S(1)} %get-tuple-element.128), channel_id=1, source_target_pairs={{0,4},{1,5},{2,6},{3,7},{4,8},{5,9},{6,10},{7,11},{8,12},{9,13},{1... | collective-permute-start | bytes 294920 | tf_op jit(solution)/shard_map/ppermute | solution.py:73
  252.4 163.0 %collective-permute-start.11 = (bf16[128,768]{1,0:T(8,128)(2,1)}, bf16[128,768]{1,0:T(8,128)(2,1)}, u32[]{:S(2)}, u32[]{:S(2)}) collective-permute-start(bf16[128,768]{1,0:T(8,128)(2,1)} %get-tuple-element.127), channel_id=1, source_target_pairs={{0,1},{1,2},{2,3},{4,5},{5,6},{6,7},{8,9},{9,10},{10,11},{12,13},{... | collective-permute-start | bytes 589832 | tf_op jit(solution)/shard_map/ppermute | solution.py:73
  259.4 155.9 %collective-permute-start.10 = (bf16[128,768]{1,0:T(8,128)(2,1)}, bf16[128,768]{1,0:T(8,128)(2,1)}, u32[]{:S(2)}, u32[]{:S(2)}) collective-permute-start(bf16[128,768]{1,0:T(8,128)(2,1)} %get-tuple-element.126), channel_id=1, source_target_pairs={{1,0},{2,1},{3,2},{5,4},{6,5},{7,6},{9,8},{10,9},{11,10},{13,12},{... | collective-permute-start | bytes 589832 | tf_op jit(solution)/shard_map/ppermute | solution.py:73
  261.4 21.2 %collective-permute-start.38 = (bf16[1536,256]{1,0:T(8,128)(2,1)}, bf16[1536,256]{1,0:T(8,128)(2,1)}, u32[]{:S(2)}, u32[]{:S(2)}) collective-permute-start(bf16[1536,256]{1,0:T(8,128)(2,1)} %dynamic-slice_bitcast_fusion.1), channel_id=1, source_target_pairs={{0,1},{1,0},{2,3},{3,2},{4,5},{5,4},{6,7},{7,6},{8,9},{9,8},{10,11... | collective-permute-start | bytes 2359304 | tf_op jit(solution)/shard_map/ppermute | solution.py:73
  262.2 21.8 %collective-permute-start.18 = (bf16[1536,256]{1,0:T(8,128)(2,1)}, bf16[1536,256]{1,0:T(8,128)(2,1)}, u32[]{:S(2)}, u32[]{:S(2)}) collective-permute-start(bf16[1536,256]{1,0:T(8,128)(2,1)} %dynamic-slice_bitcast_fusion.2), channel_id=1, source_target_pairs={{0,1},{1,0},{2,3},{3,2},{4,5},{5,4},{6,7},{7,6},{8,9},{9,8},{10,11... | collective-permute-start | bytes 2359304 | tf_op jit(solution)/shard_map/ppermute | solution.py:73
  265.1 147.6 %all-to-all-start.1 = ((bf16[64,8,768]{2,1,0:T(8,128)(2,1)}), bf16[64,8,768]{2,1,0:T(8,128)(2,1)}, u32[]{:S(2)}, u32[]{:S(2)}) async-start(bf16[64,8,768]{2,1,0:T(8,128)(2,1)} %fusion.10), calls=%async_computation.1 | async-start | bytes 1572864 | tf_op jit(solution)/shard_map/all_to_all | solution.py:162
  280.0 14.1 %collective-permute-start.61 = (bf16[384,256]{1,0:T(8,128)(2,1)S(1)}, bf16[384,256]{1,0:T(8,128)(2,1)S(1)}, u32[]{:S(2)}, u32[]{:S(2)}) collective-permute-start(bf16[384,256]{1,0:T(8,128)(2,1)S(1)} %get-tuple-element.147), channel_id=1, source_target_pairs={{0,18},{1,97},{2,16},{3,99},{4,22},{5,101},{6,20},{7,103},{8,26},{... | collective-permute-start | bytes 589832 | tf_op jit(solution)/shard_map/ppermute | solution.py:73
  282.6 13.0 %collective-permute-start.60 = (bf16[384,256]{1,0:T(8,128)(2,1)S(1)}, bf16[384,256]{1,0:T(8,128)(2,1)S(1)}, u32[]{:S(2)}, u32[]{:S(2)}) collective-permute-start(bf16[384,256]{1,0:T(8,128)(2,1)S(1)} %get-tuple-element.148), channel_id=1, source_target_pairs={{0,16},{1,33},{2,18},{3,35},{4,20},{5,37},{6,22},{7,39},{8,24},{9,... | collective-permute-start | bytes 589832 | tf_op jit(solution)/shard_map/ppermute | solution.py:73
  284.0 14.0 %collective-permute-start.59 = (bf16[384,256]{1,0:T(8,128)(2,1)S(1)}, bf16[384,256]{1,0:T(8,128)(2,1)S(1)}, u32[]{:S(2)}, u32[]{:S(2)}) collective-permute-start(bf16[384,256]{1,0:T(8,128)(2,1)S(1)} %get-tuple-element.146), channel_id=1, source_target_pairs={{0,2},{1,65},{2,0},{3,67},{4,6},{5,69},{6,4},{7,71},{8,10},{9,73},... | collective-permute-start | bytes 589832 | tf_op jit(solution)/shard_map/ppermute | solution.py:73
  294.1 5.3 collective-permute-start.41
  295.6 6.7 %collective-permute-start.40 = (bf16[384,256]{1,0:T(8,128)(2,1)S(1)}, bf16[384,256]{1,0:T(8,128)(2,1)S(1)}, u32[]{:S(2)}, u32[]{:S(2)}) collective-permute-start(bf16[384,256]{1,0:T(8,128)(2,1)S(1)} %get-tuple-element.145), channel_id=1, source_target_pairs={{0,32},{1,5},{2,34},{3,7},{4,36},{5,9},{6,38},{7,11},{8,40},{9,13}... | collective-permute-start | bytes 589832 | tf_op jit(solution)/shard_map/ppermute | solution.py:73
  297.9 8.3 %collective-permute-start.39 = (bf16[384,256]{1,0:T(8,128)(2,1)S(1)}, bf16[384,256]{1,0:T(8,128)(2,1)S(1)}, u32[]{:S(2)}, u32[]{:S(2)}) collective-permute-start(bf16[384,256]{1,0:T(8,128)(2,1)S(1)} %get-tuple-element.143), channel_id=1, source_target_pairs={{0,64},{1,9},{2,66},{3,11},{4,68},{5,13},{6,70},{7,15},{8,72},{9,1... | collective-permute-start | bytes 589832 | tf_op jit(solution)/shard_map/ppermute | solution.py:73
  299.4 7.1 %collective-permute-start.21 = (bf16[384,256]{1,0:T(8,128)(2,1)S(1)}, bf16[384,256]{1,0:T(8,128)(2,1)S(1)}, u32[]{:S(2)}, u32[]{:S(2)}) collective-permute-start(bf16[384,256]{1,0:T(8,128)(2,1)S(1)} %get-tuple-element.141), channel_id=1, source_target_pairs={{0,12},{1,19},{2,14},{3,17},{4,0},{5,23},{6,2},{7,21},{8,4},{9,27}... | collective-permute-start | bytes 589832 | tf_op jit(solution)/shard_map/ppermute | solution.py:73
  302.3 7.6 %collective-permute-start.20 = (bf16[384,256]{1,0:T(8,128)(2,1)S(1)}, bf16[384,256]{1,0:T(8,128)(2,1)S(1)}, u32[]{:S(2)}, u32[]{:S(2)}) collective-permute-start(bf16[384,256]{1,0:T(8,128)(2,1)S(1)} %get-tuple-element.142), channel_id=1, source_target_pairs={{0,4},{1,17},{2,6},{3,19},{4,8},{5,21},{6,10},{7,23},{8,12},{9,25}... | collective-permute-start | bytes 589832 | tf_op jit(solution)/shard_map/ppermute | solution.py:73
  306.3 7.1 %collective-permute-start.19 = (bf16[384,256]{1,0:T(8,128)(2,1)S(1)}, bf16[384,256]{1,0:T(8,128)(2,1)S(1)}, u32[]{:S(2)}, u32[]{:S(2)}) collective-permute-start(bf16[384,256]{1,0:T(8,128)(2,1)S(1)} %get-tuple-element.140), channel_id=1, source_target_pairs={{0,8},{1,3},{2,10},{3,1},{4,12},{5,7},{6,14},{7,5},{8,0},{9,11},{1... | collective-permute-start | bytes 589832 | tf_op jit(solution)/shard_map/ppermute | solution.py:73
  306.5 9.7 %collective-permute-start.64 = (bf16[96,256]{1,0:T(8,128)(2,1)S(1)}, bf16[96,256]{1,0:T(8,128)(2,1)S(1)}, u32[]{:S(2)}, u32[]{:S(2)}) collective-permute-start(bf16[96,256]{1,0:T(8,128)(2,1)S(1)} %get-tuple-element.156), channel_id=1, source_target_pairs={{0,12},{1,19},{2,14},{3,17},{4,0},{5,23},{6,2},{7,21},{8,4},{9,27}... | collective-permute-start | bytes 147464 | tf_op jit(solution)/shard_map/ppermute | solution.py:73
  309.9 9.2 %collective-permute-start.63 = (bf16[96,256]{1,0:T(8,128)(2,1)S(1)}, bf16[96,256]{1,0:T(8,128)(2,1)S(1)}, u32[]{:S(2)}, u32[]{:S(2)}) collective-permute-start(bf16[96,256]{1,0:T(8,128)(2,1)S(1)} %get-tuple-element.157), channel_id=1, source_target_pairs={{0,4},{1,17},{2,6},{3,19},{4,8},{5,21},{6,10},{7,23},{8,12},{9,25}... | collective-permute-start | bytes 147464 | tf_op jit(solution)/shard_map/ppermute | solution.py:73
  313.4 5.7 %collective-permute-start.62 = (bf16[96,256]{1,0:T(8,128)(2,1)S(1)}, bf16[96,256]{1,0:T(8,128)(2,1)S(1)}, u32[]{:S(2)}, u32[]{:S(2)}) collective-permute-start(bf16[96,256]{1,0:T(8,128)(2,1)S(1)} %get-tuple-element.155), channel_id=1, source_target_pairs={{0,8},{1,3},{2,10},{3,1},{4,12},{5,7},{6,14},{7,5},{8,0},{9,11},{1... | collective-permute-start | bytes 147464 | tf_op jit(solution)/shard_map/ppermute | solution.py:73
  316.2 8.2 %collective-permute-start.44 = (bf16[96,256]{1,0:T(8,128)(2,1)S(1)}, bf16[96,256]{1,0:T(8,128)(2,1)S(1)}, u32[]{:S(2)}, u32[]{:S(2)}) collective-permute-start(bf16[96,256]{1,0:T(8,128)(2,1)S(1)} %get-tuple-element.153), channel_id=1, source_target_pairs={{0,18},{1,97},{2,16},{3,99},{4,22},{5,101},{6,20},{7,103},{8,26},{... | collective-permute-start | bytes 147464 | tf_op jit(solution)/shard_map/ppermute | solution.py:73
  319.1 5.9 %collective-permute-start.43 = (bf16[96,256]{1,0:T(8,128)(2,1)S(1)}, bf16[96,256]{1,0:T(8,128)(2,1)S(1)}, u32[]{:S(2)}, u32[]{:S(2)}) collective-permute-start(bf16[96,256]{1,0:T(8,128)(2,1)S(1)} %get-tuple-element.154), channel_id=1, source_target_pairs={{0,16},{1,33},{2,18},{3,35},{4,20},{5,37},{6,22},{7,39},{8,24},{9,... | collective-permute-start | bytes 147464 | tf_op jit(solution)/shard_map/ppermute | solution.py:73
  319.1 7.3 %collective-permute-start.42 = (bf16[96,256]{1,0:T(8,128)(2,1)S(1)}, bf16[96,256]{1,0:T(8,128)(2,1)S(1)}, u32[]{:S(2)}, u32[]{:S(2)}) collective-permute-start(bf16[96,256]{1,0:T(8,128)(2,1)S(1)} %get-tuple-element.152), channel_id=1, source_target_pairs={{0,2},{1,65},{2,0},{3,67},{4,6},{5,69},{6,4},{7,71},{8,10},{9,73},... | collective-permute-start | bytes 147464 | tf_op jit(solution)/shard_map/ppermute | solution.py:73
  326.4 4.4 collective-permute-start.22
  330.8 4.7 collective-permute-start.65
  331.0 5.3 collective-permute-start.47
  336.3 5.4 collective-permute-start.27
  337.7 5.1 collective-permute-start.26
  345.8 4.5 collective-permute-start.48
  346.7 4.5 collective-permute-start.49
  354.3 4.4 collective-permute-start.71
  354.8 5.4 collective-permute-start.72
  356.3 4.8 collective-permute-start.73
  358.8 4.5 collective-permute-start.51
  361.1 4.6 collective-permute-start.53
  364.4 4.7 collective-permute-start.32
  365.6 4.5 collective-permute-start.33
  367.7 7.0 %collective-permute-start.74 = (bf16[384,256]{1,0:T(8,128)(2,1)S(1)}, bf16[384,256]{1,0:T(8,128)(2,1)S(1)}, u32[]{:S(2)}, u32[]{:S(2)}) collective-permute-start(bf16[384,256]{1,0:T(8,128)(2,1)S(1)} %bitcast.348), channel_id=1, source_target_pairs={{0,2},{1,65},{2,0},{3,67},{4,6},{5,69},{6,4},{7,71},{8,10},{9,73},... | collective-permute-start | bytes 589832 | tf_op jit(solution)/shard_map/ppermute | solution.py:73
  369.1 6.4 %collective-permute-start.75 = (bf16[384,256]{1,0:T(8,128)(2,1)S(1)}, bf16[384,256]{1,0:T(8,128)(2,1)S(1)}, u32[]{:S(2)}, u32[]{:S(2)}) collective-permute-start(bf16[384,256]{1,0:T(8,128)(2,1)S(1)} %bitcast.349), channel_id=1, source_target_pairs={{0,18},{1,97},{2,16},{3,99},{4,22},{5,101},{6,20},{7,103},{8,26},{... | collective-permute-start | bytes 589832 | tf_op jit(solution)/shard_map/ppermute | solution.py:73
  370.2 7.7 %collective-permute-start.76 = (bf16[384,256]{1,0:T(8,128)(2,1)S(1)}, bf16[384,256]{1,0:T(8,128)(2,1)S(1)}, u32[]{:S(2)}, u32[]{:S(2)}) collective-permute-start(bf16[384,256]{1,0:T(8,128)(2,1)S(1)} %bitcast.351), channel_id=1, source_target_pairs={{0,16},{1,33},{2,18},{3,35},{4,20},{5,37},{6,22},{7,39},{8,24},{9,... | collective-permute-start | bytes 589832 | tf_op jit(solution)/shard_map/ppermute | solution.py:73
  374.7 6.9 %collective-permute-start.54 = (bf16[384,256]{1,0:T(8,128)(2,1)S(1)}, bf16[384,256]{1,0:T(8,128)(2,1)S(1)}, u32[]{:S(2)}, u32[]{:S(2)}) collective-permute-start(bf16[384,256]{1,0:T(8,128)(2,1)S(1)} %bitcast.353), channel_id=1, source_target_pairs={{0,64},{1,9},{2,66},{3,11},{4,68},{5,13},{6,70},{7,15},{8,72},{9,1... | collective-permute-start | bytes 589832 | tf_op jit(solution)/shard_map/ppermute | solution.py:73
  375.5 7.3 %collective-permute-start.55 = (bf16[384,256]{1,0:T(8,128)(2,1)S(1)}, bf16[384,256]{1,0:T(8,128)(2,1)S(1)}, u32[]{:S(2)}, u32[]{:S(2)}) collective-permute-start(bf16[384,256]{1,0:T(8,128)(2,1)S(1)} %bitcast.354), channel_id=1, source_target_pairs={{0,96},{1,13},{2,98},{3,15},{4,100},{5,1},{6,102},{7,3},{8,104},{9... | collective-permute-start | bytes 589832 | tf_op jit(solution)/shard_map/ppermute | solution.py:73
  377.8 7.2 %collective-permute-start.56 = (bf16[384,256]{1,0:T(8,128)(2,1)S(1)}, bf16[384,256]{1,0:T(8,128)(2,1)S(1)}, u32[]{:S(2)}, u32[]{:S(2)}) collective-permute-start(bf16[384,256]{1,0:T(8,128)(2,1)S(1)} %bitcast.355), channel_id=1, source_target_pairs={{0,32},{1,5},{2,34},{3,7},{4,36},{5,9},{6,38},{7,11},{8,40},{9,13}... | collective-permute-start | bytes 589832 | tf_op jit(solution)/shard_map/ppermute | solution.py:73
  381.5 8.0 %collective-permute-start.34 = (bf16[384,256]{1,0:T(8,128)(2,1)S(1)}, bf16[384,256]{1,0:T(8,128)(2,1)S(1)}, u32[]{:S(2)}, u32[]{:S(2)}) collective-permute-start(bf16[384,256]{1,0:T(8,128)(2,1)S(1)} %bitcast.357), channel_id=1, source_target_pairs={{0,8},{1,3},{2,10},{3,1},{4,12},{5,7},{6,14},{7,5},{8,0},{9,11},{1... | collective-permute-start | bytes 589832 | tf_op jit(solution)/shard_map/ppermute | solution.py:73
  382.8 22.8 %collective-permute-start.35 = (bf16[384,256]{1,0:T(8,128)(2,1)S(1)}, bf16[384,256]{1,0:T(8,128)(2,1)S(1)}, u32[]{:S(2)}, u32[]{:S(2)}) collective-permute-start(bf16[384,256]{1,0:T(8,128)(2,1)S(1)} %bitcast.358), channel_id=1, source_target_pairs={{0,12},{1,19},{2,14},{3,17},{4,0},{5,23},{6,2},{7,21},{8,4},{9,27}... | collective-permute-start | bytes 589832 | tf_op jit(solution)/shard_map/ppermute | solution.py:73
  385.0 24.8 %collective-permute-start.36 = (bf16[384,256]{1,0:T(8,128)(2,1)S(1)}, bf16[384,256]{1,0:T(8,128)(2,1)S(1)}, u32[]{:S(2)}, u32[]{:S(2)}) collective-permute-start(bf16[384,256]{1,0:T(8,128)(2,1)S(1)} %bitcast.359), channel_id=1, source_target_pairs={{0,4},{1,17},{2,6},{3,19},{4,8},{5,21},{6,10},{7,23},{8,12},{9,25}... | collective-permute-start | bytes 589832 | tf_op jit(solution)/shard_map/ppermute | solution.py:73
  389.6 94.8 %collective-permute-start.77 = (bf16[1536,256]{1,0:T(8,128)(2,1)S(1)}, bf16[1536,256]{1,0:T(8,128)(2,1)}, u32[]{:S(2)}, u32[]{:S(2)}) collective-permute-start(bf16[1536,256]{1,0:T(8,128)(2,1)S(1)} %bitcast.330), channel_id=1, source_target_pairs={{0,1},{1,0},{2,3},{3,2},{4,5},{5,4},{6,7},{7,6},{8,9},{9,8},{10,11... | collective-permute-start | bytes 2359304 | tf_op jit(solution)/shard_map/ppermute | solution.py:73
  405.6 79.9 %collective-permute-start.57 = (bf16[1536,256]{1,0:T(8,128)(2,1)}, bf16[1536,256]{1,0:T(8,128)(2,1)}, u32[]{:S(2)}, u32[]{:S(2)}) collective-permute-start(bf16[1536,256]{1,0:T(8,128)(2,1)} %bitcast.107), channel_id=1, source_target_pairs={{0,1},{1,0},{2,3},{3,2},{4,5},{5,4},{6,7},{7,6},{8,9},{9,8},{10,11... | collective-permute-start | bytes 2359304 | tf_op jit(solution)/shard_map/ppermute | solution.py:73
  409.9 77.2 %collective-permute-start.37 = (bf16[1536,256]{1,0:T(8,128)(2,1)S(1)}, bf16[1536,256]{1,0:T(8,128)(2,1)}, u32[]{:S(2)}, u32[]{:S(2)}) collective-permute-start(bf16[1536,256]{1,0:T(8,128)(2,1)S(1)} %bitcast.329), channel_id=1, source_target_pairs={{0,1},{1,0},{2,3},{3,2},{4,5},{5,4},{6,7},{7,6},{8,9},{9,8},{10,11... | collective-permute-start | bytes 2359304 | tf_op jit(solution)/shard_map/ppermute | solution.py:73
  (69 other events, 406.5 us)
Sparse Core Ops, SparseCore 0:
  233.9 191.5 all-reduce.7
